TPU v7x, 512 devices: a whole 4x4x16 slice. The times are simulated.
512 devices in a mesh: head: 32 (over z_lo, y, core), seq: 16 (over z_hi, x).
Axes of the slice: x: 4, y: 4, z: 16 (z_hi: 4, z_lo: 4; z = z_hi * 4 + z_lo), core: 2. Of those that a mesh axis runs over, the one named last changes fastest.
Arguments:
- query_rows: bfloat16 [2048, 16384], P('seq', 'head'), may hold values from -512 to 512
- key_rows: bfloat16 [2048, 1024], P('seq'), may hold values from -32 to 32
- value_rows: bfloat16 [2048, 1024], P('seq'), may hold values from -6 to 6
- positions: int32 [2048], P('seq'), may hold values from 0 to 511, as said below
Outputs:
- attended: bfloat16 [2048, 16384], P('seq', 'head')
- hessian: float32 [16384, 16384], P('head', 'seq')
Inputs may be any that keep to these rules, and one draw needn't show every extreme that they name: Each aligned block of 4 spans of 128 tokens is one sequence; each span holds 128 consecutive ascending positions starting at a multiple of 128, and the sequence's spans together hold every position 0 to 511 once.
All inputs are finite; a program needn't handle non-finite values.
Results may differ from a plain program's by a relative error of at most 0.0037.
Values may be sent and summed in bfloat16 or wider, within the bound.
No kernel may reach another device: no remote copies, remote signals or barrier semaphores. Data moves between devices by JAX's collectives and lax.ppermute only.
A program may use at most 64 MiB of HBM per device.

v0:
```python
import jax
import jax.numpy as jnp
from jax import lax
from jax.sharding import PartitionSpec as P

HEADS = 128
KVH = 8
HD = 128
SPANS = 4


def from_partner(value, axis, stride):
    mask = 2**stride
    pairs = [(source, source ^ mask) for source in range(lax.axis_size(axis))]
    return lax.ppermute(value, axis, pairs)


def attend_block(queries, key_block, value_block, visible, local_heads, local_tokens, score_scale):
    scores = jnp.dot(queries, key_block.T, preferred_element_type=jnp.float32) * score_scale
    scores = scores.reshape(local_heads, local_tokens, key_block.shape[0])
    masked = jnp.where(visible[None], scores, -jnp.inf)
    row_top = jnp.max(masked, axis=2, keepdims=True)
    weights = jnp.exp(masked - row_top)
    weight_sum = jnp.sum(weights, axis=2, keepdims=True)
    mixed = jnp.dot(
        weights.astype(jnp.bfloat16).reshape(local_heads * local_tokens, key_block.shape[0]),
        value_block,
        preferred_element_type=jnp.float32,
    )
    return mixed.reshape(local_heads, local_tokens, HD) / weight_sum


def on_device(query_rows, key_rows, value_rows, positions):
    local_tokens = query_rows.shape[0]
    local_heads = query_rows.shape[1] // HD
    group_size = HEADS // KVH
    score_scale = HD ** (-0.5)
    head_index = lax.axis_index("head")
    seq_devices = lax.axis_size("seq")
    head_devices = lax.axis_size("head")
    key_head = head_index * local_heads // group_size
    key_slice = lax.dynamic_slice_in_dim(key_rows, key_head * HD, HD, 1)
    value_slice = lax.dynamic_slice_in_dim(value_rows, key_head * HD, HD, 1)
    queries = jnp.transpose(query_rows.reshape(local_tokens, local_heads, HD), (1, 0, 2))
    queries = queries.reshape(local_heads * local_tokens, HD)
    key_block, value_block, place_block = (key_slice, value_slice, positions)
    for bit in range(SPANS.bit_length() - 1):
        other_keys, other_values, other_places = from_partner(
            (key_block, value_block, place_block), "seq", bit
        )
        key_block = jnp.concatenate([key_block, other_keys], axis=0)
        value_block = jnp.concatenate([value_block, other_values], axis=0)
        place_block = jnp.concatenate([place_block, other_places], axis=0)
    visible = place_block[None, :] <= positions[:, None]
    outcome = attend_block(
        queries, key_block, value_block, visible, local_heads, local_tokens, score_scale
    )
    attended = (
        jnp.transpose(outcome, (1, 0, 2))
        .reshape(local_tokens, local_heads * HD)
        .astype(jnp.bfloat16)
    )
    row_width = attended.shape[1]
    row_operand = lax.all_gather(attended, "seq", axis=0, tiled=True)
    per_slice = local_tokens // head_devices
    sectioned = attended.reshape(1, per_slice, head_devices, row_width)
    sectioned = lax.all_to_all(sectioned, "head", split_axis=2, concat_axis=3, tiled=True)
    sectioned = lax.all_to_all(sectioned, "seq", split_axis=3, concat_axis=0, tiled=True)
    row_grid = row_operand.reshape(seq_devices, per_slice, head_devices, row_width)
    hessian = lax.dot_general(
        row_grid,
        lax.all_gather(sectioned, "head", axis=2, tiled=True),
        (((0, 1, 2), (0, 1, 2)), ((), ())),
        preferred_element_type=jnp.float32,
    )
    return (attended, hessian)


def solution(mesh):
    placed = (P("seq", "head"), P("seq", None), P("seq", None), P("seq"))
    return jax.shard_map(
        on_device,
        mesh=mesh,
        in_specs=placed,
        out_specs=(P("seq", "head"), P("head", "seq")),
        check_vma=False,
    )
```

profile of v0, /device:TPU:1, one launch (start us, length us, event | category | flops | bytes accessed | tf_op | source)
XLA Modules:
  0.0 303.3 jit_solution(11701521761003018919)
XLA Ops:
  7.2 4.1 %collective-permute-start = (s32[128]{0:T(128)}, s32[128]{0:T(128)S(1)}, u32[]{:S(2)}, u32[]{:S(2)}) collective-permute-start(s32[128]{0:T(128)} %param.7), channel_id=1, source_target_pairs={{0,1},{1,0},{2,3},{3,2},{4,5},{5,4},{6,7},{7,6},{8,9},{9,8},{10,11... | collective-permute-start | bytes 1544 | tf_op jit(solution)/shard_map/ppermute | solution.py:15
  11.4 1.9 collective-permute-start.2
  13.3 0.7 pad_add_fusion.1
  14.0 4.9 %collective-permute-start.1 = (s32[256]{0:T(256)S(1)}, s32[256]{0:T(256)S(1)}, u32[]{:S(2)}, u32[]{:S(2)}) collective-permute-start(s32[256]{0:T(256)S(1)} %pad_add_fusion.1), channel_id=1, source_target_pairs={{0,2},{1,3},{2,0},{3,1},{4,6},{5,7},{6,4},{7,5},{8,10},{9,11},{10,... | collective-permute-start | bytes 3080 | tf_op jit(solution)/shard_map/ppermute | solution.py:15
  18.9 0.8 constant_dynamic-slice_fusion
  19.6 0.1 copy.33
  19.7 2.2 collective-permute-start.4
  22.0 1.0 copy.21
  23.0 0.1 copy.22
  23.2 0.7 pad_add_fusion
  23.8 0.8 broadcast_compare_fusion
  24.6 3.6 %collective-permute-start.3 = (bf16[256,128]{1,0:T(8,128)(2,1)S(1)}, bf16[256,128]{1,0:T(8,128)(2,1)S(1)}, u32[]{:S(2)}, u32[]{:S(2)}) collective-permute-start(bf16[256,128]{1,0:T(8,128)(2,1)S(1)} %pad_maximum_fusion), channel_id=1, source_target_pairs={{0,2},{1,3},{2,0},{3,1},{4,6},{5,7},{6,4},{7,5},{8,10},{9,11},{10,... | collective-permute-start | bytes 196616 | tf_op jit(solution)/shard_map/ppermute | solution.py:15
  28.3 3.1 %collective-permute-start.5 = (bf16[256,128]{0,1:T(8,128)(2,1)S(1)}, bf16[256,128]{0,1:T(8,128)(2,1)S(1)}, u32[]{:S(2)}, u32[]{:S(2)}) collective-permute-start(bf16[256,128]{0,1:T(8,128)(2,1)S(1)} %pad_maximum_fusion.1), channel_id=1, source_target_pairs={{0,2},{1,3},{2,0},{3,1},{4,6},{5,7},{6,4},{7,5},{8,10},{9,11},{10,... | collective-permute-start | bytes 196616 | tf_op jit(solution)/shard_map/ppermute | solution.py:15
  31.6 0.4 fusion.23
  32.0 0.3 fusion.10
  32.3 2.5 collective-permute-done.5
  34.8 1.0 fusion.9
  35.8 1.0 copy.25
  36.9 0.1 copy.26
  37.1 20.3 %all_to_all.30 = bf16[1,4,32,512]{3,1,0,2:T(4,128)(2,1)S(1)} all-to-all(bf16[1,4,32,512]{3,1,0,2:T(4,128)(2,1)S(1)} %copy.26), channel_id=1, replica_groups=mesh['head'=32,'seq'=16] {'head'}, dimensions={2} | all-to-all | bytes 262144 | tf_op jit(solution)/shard_map/all_to_all | solution.py:67
  57.3 12.9 %copy.27 = bf16[1,4,1,16384]{1,2,0,3:T(2,128)(2,1)} copy(bf16[1,4,1,16384]{3,1,2,0:T(4,128)(2,1)S(1)} %bitcast.58) | data formatting | bytes 262144 | tf_op jit(solution)/shard_map/all_to_all | solution.py:67
  70.2 0.5 broadcast.33
  70.7 90.8 %reduce.2 = bf16[16384,4]{1,0:T(8,128)(2,1)} reduce(bf16[16384,1,1,4]{3,2,1,0:T(2,128)(2,1)} %bitcast.52, bf16[]{:T(256)} %broadcast.33), dimensions={1,2}, to_apply=%bitcast.45.reduce_sub_computation | reduce | bytes 262146
  161.5 8.7 %reshape.80 = bf16[16,2,2048]{2,1,0:T(2,128)(2,1)S(1)} reshape(bf16[16384,4]{1,0:T(8,128)(2,1)} %reduce.2) | data formatting | bytes 262144
  170.2 27.8 %all_to_all.31 = bf16[16,2,2048]{2,1,0:T(2,128)(2,1)S(1)} all-to-all(bf16[16,2,2048]{2,1,0:T(2,128)(2,1)S(1)} %reshape.80), channel_id=1, replica_groups=mesh['head'=32,'seq'=16] {'seq'}, dimensions={0} | all-to-all | bytes 262144 | tf_op jit(solution)/shard_map/all_to_all | solution.py:68
  198.0 12.3 %reshape.81 = bf16[16384,1,1,4]{3,2,1,0:T(2,128)(2,1)} reshape(bf16[16,2,2048]{2,1,0:T(2,128)(2,1)S(1)} %all_to_all.31) | data formatting | bytes 262144
  210.3 15.4 %copy.28 = bf16[1,4,1,16384]{3,1,2,0:T(4,128)(2,1)S(1)} copy(bf16[1,4,1,16384]{1,2,0,3:T(2,128)(2,1)} %bitcast.53) | data formatting | bytes 262144 | tf_op jit(solution)/shard_map/all_to_all | solution.py:68
  225.7 0.7 copy.42
  226.4 0.8 copy.31
  227.2 2.9 copy.24
  230.1 57.4 %all-gather.6.cloned.1.call-done = bf16[16,1,4,32,1024]{4,0,2,1,3:T(8,128)(2,1)} async-done(((bf16[16,1,4,1,1024]{4,0,2,1,3:T(8,128)(2,1)}), bf16[16,1,4,32,1024]{4,0,2,1,3:T(8,128)(2,1)}) %all-gather.6.cloned.1.call-update) | async-done | bytes 4194320 | tf_op jit(solution)/shard_map/all_gather | solution.py:72
  287.5 9.0 %fusion.3 = f32[512,1024]{1,0:T(8,128)} fusion(bf16[16,4,32,512]{3,2,1,0:T(8,128)(2,1)S(1)} %bitcast.54, bf16[16,1,4,32,1024]{4,0,2,1,3:T(8,128)(2,1)} %all-gather.6.cloned.1.call-done), kind=kOutput, calls=%fused_computation.3 | convolution fusion | flops 2147483648 | bytes 8388608 | tf_op jit(solution)/shard_map/dot_general | solution.py:70
  (19 shorter events, 0.3 us)
Async XLA Ops:
  7.2 4.2 %copy-start = (bf16[128,1024]{1,0:T(8,128)(2,1)S(1)}, bf16[128,1024]{1,0:T(8,128)(2,1)}, u32[]{:S(2)}) copy-start(bf16[128,1024]{1,0:T(8,128)(2,1)} %param.5) | copy-start | bytes 786436
  7.2 220.0 %all-gather.4.cloned.1.call-start = ((), (), s32[]{:S(2)}) async-start(), calls=%async_computation.2 | async-start | bytes 2228224 | tf_op jit(solution)/shard_map/all_gather | solution.py:64
  7.2 6.1 %collective-permute-start = (s32[128]{0:T(128)}, s32[128]{0:T(128)S(1)}, u32[]{:S(2)}, u32[]{:S(2)}) collective-permute-start(s32[128]{0:T(128)} %param.7), channel_id=1, source_target_pairs={{0,1},{1,0},{2,3},{3,2},{4,5},{5,4},{6,7},{7,6},{8,9},{9,8},{10,11... | collective-permute-start | bytes 1544 | tf_op jit(solution)/shard_map/ppermute | solution.py:15
  11.4 13.2 %collective-permute-start.2 = (bf16[128,128]{1,0:T(8,128)(2,1)S(1)}, bf16[128,128]{1,0:T(8,128)(2,1)S(1)}, u32[]{:S(2)}, u32[]{:S(2)}) collective-permute-start(bf16[128,128]{1,0:T(8,128)(2,1)S(1)} %constant_dynamic-slice_fusion.1), channel_id=1, source_target_pairs={{0,1},{1,0},{2,3},{3,2},{4,5},{5,4},{6,7},{7,6},{8,9},{9,8},{10,11... | collective-permute-start | bytes 98312 | tf_op jit(solution)/shard_map/ppermute | solution.py:15
  14.0 9.2 %collective-permute-start.1 = (s32[256]{0:T(256)S(1)}, s32[256]{0:T(256)S(1)}, u32[]{:S(2)}, u32[]{:S(2)}) collective-permute-start(s32[256]{0:T(256)S(1)} %pad_add_fusion.1), channel_id=1, source_target_pairs={{0,2},{1,3},{2,0},{3,1},{4,6},{5,7},{6,4},{7,5},{8,10},{9,11},{10,... | collective-permute-start | bytes 3080 | tf_op jit(solution)/shard_map/ppermute | solution.py:15
  19.7 8.5 %collective-permute-start.4 = (bf16[128,128]{0,1:T(8,128)(2,1)S(1)}, bf16[128,128]{0,1:T(8,128)(2,1)S(1)}, u32[]{:S(2)}, u32[]{:S(2)}) collective-permute-start(bf16[128,128]{0,1:T(8,128)(2,1)S(1)} %copy.33), channel_id=1, source_target_pairs={{0,1},{1,0},{2,3},{3,2},{4,5},{5,4},{6,7},{7,6},{8,9},{9,8},{10,11... | collective-permute-start | bytes 98312 | tf_op jit(solution)/shard_map/ppermute | solution.py:15
  24.6 6.9 %collective-permute-start.3 = (bf16[256,128]{1,0:T(8,128)(2,1)S(1)}, bf16[256,128]{1,0:T(8,128)(2,1)S(1)}, u32[]{:S(2)}, u32[]{:S(2)}) collective-permute-start(bf16[256,128]{1,0:T(8,128)(2,1)S(1)} %pad_maximum_fusion), channel_id=1, source_target_pairs={{0,2},{1,3},{2,0},{3,1},{4,6},{5,7},{6,4},{7,5},{8,10},{9,11},{10,... | collective-permute-start | bytes 196616 | tf_op jit(solution)/shard_map/ppermute | solution.py:15
  28.3 6.5 %collective-permute-start.5 = (bf16[256,128]{0,1:T(8,128)(2,1)S(1)}, bf16[256,128]{0,1:T(8,128)(2,1)S(1)}, u32[]{:S(2)}, u32[]{:S(2)}) collective-permute-start(bf16[256,128]{0,1:T(8,128)(2,1)S(1)} %pad_maximum_fusion.1), channel_id=1, source_target_pairs={{0,2},{1,3},{2,0},{3,1},{4,6},{5,7},{6,4},{7,5},{8,10},{9,11},{10,... | collective-permute-start | bytes 196616 | tf_op jit(solution)/shard_map/ppermute | solution.py:15
  35.8 251.7 %all-gather.6.cloned.1.call-start = ((), (), s32[]{:S(2)}) async-start(), calls=%async_computation.3 | async-start | bytes 4325376 | tf_op jit(solution)/shard_map/all_gather | solution.py:72
  210.3 16.1 %copy-start.1 = (bf16[128,4,128]{0,2,1:T(8,128)(2,1)S(1)}, bf16[128,4,128]{0,2,1:T(8,128)(2,1)}, u32[]{:S(2)}) copy-start(bf16[128,4,128]{0,2,1:T(8,128)(2,1)} %fusion.9) | copy-start | bytes 393220
Sparse Core Ops, SparseCore 0:
  35.9 105.3 all-gather.3
  226.5 60.8 all-gather.5
where the time goes:
time: 304 us; the launch traced here: 303 us
  other arithmetic  93.2 us (31%)
  waiting for transfers between devices  60 us (20%)
  local copies, waits for them, and re-layouts  57.5 us (19%)
  blocking collectives  48.1 us (16%)
  starting transfers between devices  20 us (7%)
  between operations  14.3 us (5%)
  matrix products  10.4 us (3%)
    unnamed x1, other arithmetic  90.8 us
    all_gather x1, waiting for transfers between devices, on_device(): lax.all_gather(sectioned, 'head', axis=2, tiled=True)  57.4 us
    all_to_all x1, blocking collectives, on_device(): lax.all_to_all(sectioned, 'seq', split_axis=3, concat_axis=0, tiled=True)  27.8 us
    unnamed x11, local copies, waits for them, and re-layouts  24.1 us
    all_to_all x1, blocking collectives, on_device(): lax.all_to_all(sectioned, 'head', split_axis=2, concat_axis=3, tiled=True)  20.3 us
    ppermute x6, starting transfers between devices, from_partner(): return lax.ppermute(value, axis, pairs)  19.9 us
    all_to_all x1, local copies, waits for them, and re-layouts, on_device(): lax.all_to_all(sectioned, 'seq', split_axis=3, concat_axis=0, tiled=True)  15.4 us
    all_to_all x1, local copies, waits for them, and re-layouts, on_device(): lax.all_to_all(sectioned, 'head', split_axis=2, concat_axis=3, tiled=True)  12.9 us
  transfers between devices with their start and end apart: 8, of which 2 were waited for; matrix products, arithmetic and copies ran while one was open for 50% of the time, Pallas kernels for 0%

commit v1 on v0

--- a/solution.py
+++ b/solution.py
@@ -69,7 +69,9 @@
     row_grid = row_operand.reshape(seq_devices, per_slice, head_devices, row_width)
     hessian = lax.dot_general(
         row_grid,
-        lax.all_gather(sectioned, "head", axis=2, tiled=True),
+        jnp.concatenate(
+            lax.all_to_all(jnp.stack([sectioned] * lax.axis_size("head")), "head", 0, 0), axis=2
+        ),
         (((0, 1, 2), (0, 1, 2)), ((), ())),
         preferred_element_type=jnp.float32,
     )

time: 304 us -> 386 us (1.27)
  waiting for transfers between devices: 60 us -> 134 us
  starting transfers between devices: 20 us -> 27.7 us
    all_gather x1, waiting for transfers between devices: 0.01 us -> 113 us  [on_device(): row_operand = lax.all_gather(attended, 'seq', axis=0, tiled=True)]
    all_gather x1 -> x0, waiting for transfers between devices: 57.4 us -> none  [on_device(): lax.all_gather(sectioned, 'head', axis=2, tiled=True)]
    all_to_all x0 -> x1, waiting for transfers between devices: none -> 17.7 us  [on_device(): lax.all_to_all(jnp.stack([sectioned] * lax.axis_size('head')), 'head', 0, 0)]
    all_to_all x0 -> x1, starting transfers between devices: none -> 7.79 us  [on_device(): lax.all_to_all(jnp.stack([sectioned] * lax.axis_size('head')), 'head', 0, 0)]
    another operation x0 -> x2, local copies, waits for them, and re-layouts: none -> 4.05 us  [on_device(): jnp.stack([sectioned] * lax.axis_size('head'))]
    unnamed x11 -> x13, local copies, waits for them, and re-layouts: 24.1 us -> 23.5 us
  transfers between devices with their start and end apart: 8 -> 8, of which waited for: 2 -> 3; matrix products, arithmetic and copies ran while one was open for 50% -> 2% of each run, Pallas kernels for 0% -> 0%
where the time goes in v1:
time: 386 us; the launch traced here: 385 us
  waiting for transfers between devices  134 us (35%)
  other arithmetic  93.2 us (24%)
  local copies, waits for them, and re-layouts  59.9 us (16%)
  blocking collectives  48.1 us (12%)
  starting transfers between devices  27.7 us (7%)
  between operations  14.3 us (4%)
  matrix products  7.23 us (2%)
    all_gather x1, waiting for transfers between devices, on_device(): row_operand = lax.all_gather(attended, 'seq', axis=0, tiled=True)  113 us
    unnamed x1, other arithmetic  90.8 us
    all_to_all x1, blocking collectives, on_device(): lax.all_to_all(sectioned, 'seq', split_axis=3, concat_axis=0, tiled=True)  27.8 us
    unnamed x13, local copies, waits for them, and re-layouts  23.5 us
    all_to_all x1, blocking collectives, on_device(): lax.all_to_all(sectioned, 'head', split_axis=2, concat_axis=3, tiled=True)  20.3 us
    ppermute x6, starting transfers between devices, from_partner(): return lax.ppermute(value, axis, pairs)  19.9 us
    all_to_all x1, waiting for transfers between devices, on_device(): lax.all_to_all(jnp.stack([sectioned] * lax.axis_size('head')), 'head', 0, 0)  17.7 us
    all_to_all x1, local copies, waits for them, and re-layouts, on_device(): lax.all_to_all(sectioned, 'seq', split_axis=3, concat_axis=0, tiled=True)  15.4 us
  transfers between devices with their start and end apart: 8, of which 3 were waited for; matrix products, arithmetic and copies ran while one was open for 2% of the time, Pallas kernels for 0%

profile of v1, /device:TPU:1, one launch (start us, length us, event | category | flops | bytes accessed | tf_op | source)
XLA Modules:
  0.0 384.7 jit_solution(6171439715383217816)
XLA Ops:
  7.2 4.1 %collective-permute-start = (s32[128]{0:T(128)}, s32[128]{0:T(128)S(1)}, u32[]{:S(2)}, u32[]{:S(2)}) collective-permute-start(s32[128]{0:T(128)} %param.7), channel_id=1, source_target_pairs={{0,1},{1,0},{2,3},{3,2},{4,5},{5,4},{6,7},{7,6},{8,9},{9,8},{10,11... | collective-permute-start | bytes 1544 | tf_op jit(solution)/shard_map/ppermute | solution.py:15
  11.3 1.9 collective-permute-start.2
  13.3 0.7 pad_add_fusion.1
  13.9 4.9 %collective-permute-start.1 = (s32[256]{0:T(256)S(1)}, s32[256]{0:T(256)S(1)}, u32[]{:S(2)}, u32[]{:S(2)}) collective-permute-start(s32[256]{0:T(256)S(1)} %pad_add_fusion.1), channel_id=1, source_target_pairs={{0,2},{1,3},{2,0},{3,1},{4,6},{5,7},{6,4},{7,5},{8,10},{9,11},{10,... | collective-permute-start | bytes 3080 | tf_op jit(solution)/shard_map/ppermute | solution.py:15
  18.8 0.8 constant_dynamic-slice_fusion
  19.7 2.2 collective-permute-start.4
  21.9 1.0 copy.21
  23.1 0.7 pad_add_fusion
  23.8 0.8 broadcast_compare_fusion
  24.6 3.6 collective-permute-start.3
  28.2 3.1 collective-permute-start.5
  31.5 0.4 fusion.23
  31.9 0.3 fusion.10
  32.2 2.5 collective-permute-done.5
  34.8 0.3 fusion.9
  35.1 0.1 copy.25
  35.4 20.3 %all_to_all.32 = bf16[1,4,32,512]{3,1,0,2:T(4,128)(2,1)S(1)} all-to-all(bf16[1,4,32,512]{3,1,0,2:T(4,128)(2,1)S(1)} %copy.26), channel_id=1, replica_groups=mesh['head'=32,'seq'=16] {'head'}, dimensions={2} | all-to-all | bytes 262144 | tf_op jit(solution)/shard_map/all_to_all | solution.py:67
  55.7 12.9 %copy.27 = bf16[1,4,1,16384]{1,2,0,3:T(2,128)(2,1)} copy(bf16[1,4,1,16384]{3,1,2,0:T(4,128)(2,1)S(1)} %bitcast.60) | data formatting | bytes 262144 | tf_op jit(solution)/shard_map/all_to_all | solution.py:67
  68.5 0.5 broadcast.35
  69.0 90.8 %reduce.2 = bf16[16384,4]{1,0:T(8,128)(2,1)} reduce(bf16[16384,1,1,4]{3,2,1,0:T(2,128)(2,1)} %bitcast.54, bf16[]{:T(256)} %broadcast.35), dimensions={1,2}, to_apply=%bitcast.47.reduce_sub_computation | reduce | bytes 262146
  159.8 8.7 %reshape.92 = bf16[16,2,2048]{2,1,0:T(2,128)(2,1)S(1)} reshape(bf16[16384,4]{1,0:T(8,128)(2,1)} %reduce.2) | data formatting | bytes 262144
  168.5 27.8 %all_to_all.33 = bf16[16,2,2048]{2,1,0:T(2,128)(2,1)S(1)} all-to-all(bf16[16,2,2048]{2,1,0:T(2,128)(2,1)S(1)} %reshape.92), channel_id=1, replica_groups=mesh['head'=32,'seq'=16] {'seq'}, dimensions={0} | all-to-all | bytes 262144 | tf_op jit(solution)/shard_map/all_to_all | solution.py:68
  196.3 12.3 %reshape.93 = bf16[16384,1,1,4]{3,2,1,0:T(2,128)(2,1)} reshape(bf16[16,2,2048]{2,1,0:T(2,128)(2,1)S(1)} %all_to_all.33) | data formatting | bytes 262144
  208.6 15.4 %copy.28 = bf16[1,4,1,16384]{3,1,2,0:T(4,128)(2,1)S(1)} copy(bf16[1,4,1,16384]{1,2,0,3:T(2,128)(2,1)} %bitcast.55) | data formatting | bytes 262144 | tf_op jit(solution)/shard_map/all_to_all | solution.py:68
  224.2 3.9 %stack.5 = bf16[32,16,4,1,1024]{4,2,1,3,0:T(4,128)(2,1)} broadcast(bf16[16,4,1024]{2,1,0:T(4,128)(2,1)S(1)} %copy.29), dimensions={1,2,4} | broadcast | bytes 4325376 | tf_op jit(solution)/shard_map/stack | solution.py:73
  228.1 7.8 %all-to-all-start.2 = ((bf16[32,16,4,1,1024]{4,2,1,3,0:T(4,128)(2,1)}), bf16[32,16,4,1,1024]{4,2,1,3,0:T(4,128)(2,1)}, u32[]{:S(2)}, u32[]{:S(2)}) async-start(bf16[32,16,4,1,1024]{4,2,1,3,0:T(4,128)(2,1)} %stack.5), calls=%async_computation.2 | async-start | bytes 8388608 | tf_op jit(solution)/shard_map/all_to_all | solution.py:73
  236.0 0.7 all-gather.2.cloned.1.call-update
  236.7 0.8 copy.31
  237.4 113.3 %all-gather.2.cloned.1.call-done = bf16[2048,512]{0,1:T(8,128)(2,1)} async-done(((bf16[128,512]{0,1:T(8,128)(2,1)}), bf16[2048,512]{0,1:T(8,128)(2,1)}) %all-gather.2.cloned.1.call-update) | async-done | bytes 2097168 | tf_op jit(solution)/shard_map/all_gather | solution.py:64
  350.7 2.9 copy.24
  353.6 17.7 %all-to-all-done.2 = bf16[32,16,4,1,1024]{4,2,1,3,0:T(4,128)(2,1)} async-done(((bf16[32,16,4,1,1024]{4,2,1,3,0:T(4,128)(2,1)}), bf16[32,16,4,1,1024]{4,2,1,3,0:T(4,128)(2,1)}, u32[]{:S(2)}, u32[]{:S(2)}) %all-to-all-start.2) | async-done | bytes 4194336 | tf_op jit(solution)/shard_map/all_to_all | solution.py:73
  371.3 6.5 %fusion.3 = f32[512,1024]{1,0:T(8,128)} fusion(bf16[16,4,32,512]{3,2,1,0:T(8,128)(2,1)S(1)} %bitcast.56, bf16[32,16,4,1,1024]{4,2,1,3,0:T(4,128)(2,1)} %all-to-all-done.2), kind=kOutput, calls=%fused_computation.3 | convolution fusion | flops 2147483648 | bytes 8388608 | tf_op jit(solution)/shard_map/dot_general | solution.py:70
  (22 shorter events, 0.8 us)
Async XLA Ops:
  7.2 4.1 %copy-start = (bf16[128,1024]{1,0:T(8,128)(2,1)S(1)}, bf16[128,1024]{1,0:T(8,128)(2,1)}, u32[]{:S(2)}) copy-start(bf16[128,1024]{1,0:T(8,128)(2,1)} %param.5) | copy-start | bytes 786436
  7.2 6.1 %collective-permute-start = (s32[128]{0:T(128)}, s32[128]{0:T(128)S(1)}, u32[]{:S(2)}, u32[]{:S(2)}) collective-permute-start(s32[128]{0:T(128)} %param.7), channel_id=1, source_target_pairs={{0,1},{1,0},{2,3},{3,2},{4,5},{5,4},{6,7},{7,6},{8,9},{9,8},{10,11... | collective-permute-start | bytes 1544 | tf_op jit(solution)/shard_map/ppermute | solution.py:15
  11.3 13.2 %collective-permute-start.2 = (bf16[128,128]{1,0:T(8,128)(2,1)S(1)}, bf16[128,128]{1,0:T(8,128)(2,1)S(1)}, u32[]{:S(2)}, u32[]{:S(2)}) collective-permute-start(bf16[128,128]{1,0:T(8,128)(2,1)S(1)} %constant_dynamic-slice_fusion.1), channel_id=1, source_target_pairs={{0,1},{1,0},{2,3},{3,2},{4,5},{5,4},{6,7},{7,6},{8,9},{9,8},{10,11... | collective-permute-start | bytes 98312 | tf_op jit(solution)/shard_map/ppermute | solution.py:15
  13.9 9.2 %collective-permute-start.1 = (s32[256]{0:T(256)S(1)}, s32[256]{0:T(256)S(1)}, u32[]{:S(2)}, u32[]{:S(2)}) collective-permute-start(s32[256]{0:T(256)S(1)} %pad_add_fusion.1), channel_id=1, source_target_pairs={{0,2},{1,3},{2,0},{3,1},{4,6},{5,7},{6,4},{7,5},{8,10},{9,11},{10,... | collective-permute-start | bytes 3080 | tf_op jit(solution)/shard_map/ppermute | solution.py:15
  19.7 8.5 %collective-permute-start.4 = (bf16[128,128]{0,1:T(8,128)(2,1)S(1)}, bf16[128,128]{0,1:T(8,128)(2,1)S(1)}, u32[]{:S(2)}, u32[]{:S(2)}) collective-permute-start(bf16[128,128]{0,1:T(8,128)(2,1)S(1)} %copy.33), channel_id=1, source_target_pairs={{0,1},{1,0},{2,3},{3,2},{4,5},{5,4},{6,7},{7,6},{8,9},{9,8},{10,11... | collective-permute-start | bytes 98312 | tf_op jit(solution)/shard_map/ppermute | solution.py:15
  24.6 6.9 %collective-permute-start.3 = (bf16[256,128]{1,0:T(8,128)(2,1)S(1)}, bf16[256,128]{1,0:T(8,128)(2,1)S(1)}, u32[]{:S(2)}, u32[]{:S(2)}) collective-permute-start(bf16[256,128]{1,0:T(8,128)(2,1)S(1)} %pad_maximum_fusion), channel_id=1, source_target_pairs={{0,2},{1,3},{2,0},{3,1},{4,6},{5,7},{6,4},{7,5},{8,10},{9,11},{10,... | collective-permute-start | bytes 196616 | tf_op jit(solution)/shard_map/ppermute | solution.py:15
  28.2 6.5 %collective-permute-start.5 = (bf16[256,128]{0,1:T(8,128)(2,1)S(1)}, bf16[256,128]{0,1:T(8,128)(2,1)S(1)}, u32[]{:S(2)}, u32[]{:S(2)}) collective-permute-start(bf16[256,128]{0,1:T(8,128)(2,1)S(1)} %pad_maximum_fusion.1), channel_id=1, source_target_pairs={{0,2},{1,3},{2,0},{3,1},{4,6},{5,7},{6,4},{7,5},{8,10},{9,11},{10,... | collective-permute-start | bytes 196616 | tf_op jit(solution)/shard_map/ppermute | solution.py:15
  35.1 33.5 %copy-start.1 = (bf16[128,4,128]{0,2,1:T(8,128)(2,1)}, bf16[128,4,128]{0,2,1:T(8,128)(2,1)S(1)}, u32[]{:S(2)}) copy-start(bf16[128,4,128]{0,2,1:T(8,128)(2,1)S(1)} %fusion.9) | copy-start | bytes 393220
  228.1 8.5 %copy-start.2 = (bf16[128,4,128]{0,2,1:T(8,128)(2,1)S(1)}, bf16[128,4,128]{0,2,1:T(8,128)(2,1)}, u32[]{:S(2)}) copy-start(bf16[128,4,128]{0,2,1:T(8,128)(2,1)} %copy-done.1) | copy-start | bytes 393220
  228.1 143.2 %all-to-all-start.2 = ((bf16[32,16,4,1,1024]{4,2,1,3,0:T(4,128)(2,1)}), bf16[32,16,4,1,1024]{4,2,1,3,0:T(4,128)(2,1)}, u32[]{:S(2)}, u32[]{:S(2)}) async-start(bf16[32,16,4,1,1024]{4,2,1,3,0:T(4,128)(2,1)} %stack.5), calls=%async_computation.2 | async-start | bytes 8388608 | tf_op jit(solution)/shard_map/all_to_all | solution.py:73
  235.9 114.8 %all-gather.2.cloned.1.call-start = ((), (), s32[]{:S(2)}) async-start(), calls=%async_computation.3 | async-start | bytes 2228224 | tf_op jit(solution)/shard_map/all_gather | solution.py:64
Sparse Core Ops, SparseCore 0:
  240.3 110.3 all-gather.1
